TPU v7x, 128 devices: a whole 4x4x4 slice. The times are simulated.
128 devices in a mesh: aux: 16 (over x, z), bas: 8 (over y, core).
Axes of the slice: x: 4, y: 4, z: 4, core: 2. Of those that a mesh axis runs over, the one named last changes fastest.
Arguments:
- integrals: bfloat16 [30720, 384, 128], P('aux', 'bas'), as said below
- coefficients: bfloat16 [128, 64], replicated, may hold values from -0.875 to 0.875
- supports: int32 [64, 3], replicated, may hold values from 0 to 7, all different within a row
- tile_pattern: int32 [240, 24], P('aux', 'bas'), may hold values 0 or 1
Outputs:
- exchange_matrix: float32 [384, 384], P(('aux', 'bas'))
Inputs may be any that keep to these rules, and one draw needn't show every extreme that they name: `supports`: each row names 3 different tiles. `integrals`: entries lie within 8 / sqrt(1966080) of zero.
All inputs are finite; a program needn't handle non-finite values. No bound on the sum of `tile_pattern` on one device may be relied on, other than what follows from the above.
Results may differ from a plain program's by a relative error of at most 0.0003.
Values may be sent and summed in bfloat16 or wider, within the bound.
A program may use at most 192 MiB of HBM per device.

v0:
```python
import jax
import jax.numpy as jnp
from jax import lax
from jax.sharding import PartitionSpec as P

AUX_TILE = 128
BAS_TILE = 16


def body(integrals, coefficients, supports, tile_pattern):
    span = integrals.shape[2]
    tile_of = jnp.arange(span) // BAS_TILE
    supported = jnp.any(tile_of[:, None, None] == supports[None, :, :], axis=2)
    orbitals = jnp.where(supported, coefficients, jnp.zeros_like(coefficients))
    screening = jnp.repeat(jnp.repeat(tile_pattern, BAS_TILE, axis=1), AUX_TILE, axis=0).astype(
        jnp.float32
    )
    transformed = jnp.einsum("pmn,ni->pim", integrals, orbitals, preferred_element_type=jnp.float32)
    transformed = (transformed * screening[:, None, :]).astype(jnp.bfloat16)
    contract = (((0,), (0,)), ((), ()))
    redistributed = lax.all_to_all(transformed, "bas", split_axis=1, concat_axis=2, tiled=True)
    window_rows = redistributed.shape[2]
    stacked = redistributed.reshape(-1, window_rows)
    return lax.psum_scatter(
        lax.dot_general(stacked, stacked, contract, preferred_element_type=jnp.float32),
        ("aux", "bas"),
        scatter_dimension=0,
        tiled=True,
    )


def solution(mesh):
    in_specs = (P("aux", "bas", None), P(), P(), P("aux", "bas"))
    out_specs = P(("aux", "bas"), None)
    return jax.shard_map(body, mesh=mesh, in_specs=in_specs, out_specs=out_specs, check_vma=False)
```

profile of v0, /device:TPU:1, one launch (start us, length us, event | category | flops | bytes accessed | tf_op | source)
XLA Modules:
  0.0 430.1 jit_solution(16751255514285005322)
XLA Ops:
  6.5 0.0 all-reduce.3.cloned.1.call-start
  6.5 0.7 convert_element_type.21
  7.2 0.2 broadcast_in_dim.14
  7.4 0.1 copy.23
  7.5 0.8 compare_reduce_fusion
  8.3 23.6 %fusion.2 = bf16[1920,64,48]{0,1,2:T(8,128)(2,1)} fusion(f32[1920,48]{0,1:T(8,128)S(1)} %bitcast.21, bf16[1920,48,128]{2,1,0:T(8,128)(2,1)} %param.4, pred[128,64]{0,1:T(8,128)(4,1)S(1)} %compare_reduce_fusion, bf16[128,64]{0,1:T(8,128)(2,1)} %param.5), kind=kOutput, calls=%fused_computation.3 | convolution fusion | flops 1521754112 | bytes 35782656 | tf_op jit(solution)/shard_map/pmn,ni->pim/dot_general | solution.py:18
  31.9 9.0 %copy.15 = bf16[1920,64,48]{0,2,1:T(8,128)(2,1)S(1)} copy(bf16[1920,64,48]{0,1,2:T(8,128)(2,1)} %fusion.2) | data formatting | bytes 23592960 | tf_op jit(solution)/shard_map/convert_element_type | solution.py:19
  40.9 137.9 %all_to_all.15 = bf16[1920,64,48]{0,2,1:T(8,128)(2,1)} all-to-all(bf16[1920,64,48]{0,2,1:T(8,128)(2,1)S(1)} %copy.15), channel_id=1, replica_groups=mesh['aux'=16,'bas'=8] {'bas'}, dimensions={1} | all-to-all | bytes 23592960 | tf_op jit(solution)/shard_map/all_to_all | solution.py:21
  178.8 41.9 %copy.16 = bf16[1920,8,8,48]{3,1,2,0:T(8,128)(2,1)} copy(bf16[1920,8,8,48]{0,3,2,1:T(8,128)(2,1)} %bitcast.19) | data formatting | bytes 23592960 | tf_op jit(solution)/shard_map/all_to_all | solution.py:21
  220.7 40.0 %reshape.27 = bf16[15360,384]{1,0:T(8,128)(2,1)} reshape(bf16[1920,8,8,48]{3,2,1,0:T(8,128)(2,1)} %bitcast.18) | data formatting | bytes 23592960 | tf_op jit(solution)/shard_map/reshape | solution.py:23
  260.6 15.0 %fusion.9 = f32[384,384]{1,0:T(8,128)} fusion(bf16[15360,384]{1,0:T(8,128)(2,1)} %reshape.27), kind=kOutput, calls=%fused_computation.15 | convolution fusion | flops 4529848320 | bytes 12386304 | tf_op jit(solution)/shard_map/dot_general | solution.py:25
  275.6 0.0 all-reduce.3.cloned.1.call-update
  275.7 146.2 %all-reduce.3.cloned.1.call-done = f32[384,384]{1,0:T(8,128)} async-done(((f32[384,384]{1,0:T(8,128)}), f32[384,384]{1,0:T(8,128)}) %all-reduce.3.cloned.1.call-update) | async-done | bytes 589840
  421.9 1.3 constant_dynamic-slice_fusion
  (2 shorter events, 0.0 us)
Async XLA Ops:
  6.5 415.4 %all-reduce.3.cloned.1.call-start = ((), (), s32[]{:S(2)}) async-start(), calls=%async_computation.1 | async-start | bytes 1179648
Sparse Core Ops, SparseCore 0:
  275.8 146.0 all-reduce.2
where the time goes:
time: 432 us; the launch traced here: 430 us
  waiting for transfers between devices  146 us (34%)
  blocking collectives  138 us (32%)
  local copies, waits for them, and re-layouts  92.5 us (21%)
  matrix products  38.6 us (9%)
  between operations  13.4 us (3%)
    unnamed x2, waiting for transfers between devices  146 us
    all_to_all x1, blocking collectives, body(): lax.all_to_all(transformed, 'bas', split_axis=1, concat_axis=2, tiled=True)  138 us
    all_to_all x1, local copies, waits for them, and re-layouts, body(): lax.all_to_all(transformed, 'bas', split_axis=1, concat_axis=2, tiled=True)  41.9 us
    reshape x1, local copies, waits for them, and re-layouts, body(): stacked = redistributed.reshape(-1, window_rows)  40 us
    dot_general x1, matrix products, body(): jnp.einsum('pmn,ni->pim', integrals, orbitals, preferred_element_type=jnp...  23.6 us
    dot_general x1, matrix products, body(): lax.dot_general(stacked, stacked, contract, preferred_element_type=jnp.fl...  15 us
    convert_element_type x1, local copies, waits for them, and re-layouts, body(): transformed = (transformed * screening[:, None, :]).astype(jnp.bfloat16)  9.01 us
  transfers between devices with their start and end apart: 1, of which 1 were waited for; matrix products, arithmetic and copies ran while one was open for 0% of the time, Pallas kernels for 0%

commit v1 on v0

--- a/solution.py
+++ b/solution.py
@@ -1,13 +1,25 @@
+import functools
+
 import jax
 import jax.numpy as jnp
 from jax import lax
+from jax.experimental import pallas as pl
+from jax.experimental.pallas import tpu as pltpu
 from jax.sharding import PartitionSpec as P
 
 AUX_TILE = 128
 BAS_TILE = 16
-
-
-def body(integrals, coefficients, supports, tile_pattern):
+ORBITALS = 64
+SPAN = 128
+MESH = pl.DeviceIdType.MESH
+
+CAP = 31
+SPARE = 8
+STAGES = (1, 2, 4, 4, 4, 4, 4, 4, 4)
+HANDOVER_AFTER = 2
+
+
+def dense_body(integrals, coefficients, supports, tile_pattern):
     span = integrals.shape[2]
     tile_of = jnp.arange(span) // BAS_TILE
     supported = jnp.any(tile_of[:, None, None] == supports[None, :, :], axis=2)
@@ -29,7 +41,368 @@
     )
 
 
+def kernel(
+    n_aux,
+    n_bas,
+    tiles,
+    blocks,
+    pattern_smem,
+    pattern_vmem,
+    supports_ref,
+    coefficients_ref,
+    integrals_ref,
+    out_ref,
+    flag_ref,
+    loaded,
+    weights,
+    send_buf,
+    recv_buf,
+    spare_out,
+    spare_in,
+    dense,
+    partial,
+    partial_in,
+    summed,
+    summed_in,
+    pattern_out,
+    pattern_in,
+    pattern_all,
+    following,
+    listed,
+    load_sem,
+    pattern_send,
+    pattern_recv,
+    pattern_local,
+    send_sem,
+    recv_sem,
+    own_sem,
+    spare_send,
+    spare_recv,
+    aux_send,
+    aux_recv,
+    bas_send,
+    bas_recv,
+):
+    my_aux = lax.axis_index("aux")
+    me = lax.axis_index("bas")
+    sibling = me + 1 - 2 * lax.rem(me, 2)
+    count = tiles * blocks
+    rows = AUX_TILE // n_bas // 2 * BAS_TILE
+
+    loads = []
+    for q in range(tiles):
+        loads.append(
+            pltpu.make_async_copy(integrals_ref.at[q], loaded.at[q], load_sem.at[q])
+        )
+        loads[-1].start()
+
+    barrier = pltpu.get_barrier_semaphore()
+    for k in range(1, n_bas):
+        pl.semaphore_signal(
+            barrier, inc=1, device_id={"bas": lax.rem(me + k, n_bas)}, device_id_type=MESH
+        )
+    for k in range(1, n_aux):
+        pl.semaphore_signal(
+            barrier, inc=1, device_id={"aux": lax.rem(my_aux + k, n_aux)}, device_id_type=MESH
+        )
+
+    following[count] = jnp.int32(count - 1)
+    upcoming = jnp.int32(count - 1)
+    for at in reversed(range(count)):
+        upcoming = jnp.where(pattern_smem[at % blocks, at // blocks] > 0, at, upcoming)
+        following[at] = upcoming
+    at = following[0]
+    for s in range(CAP + SPARE):
+        listed[s] = at
+        at = following[at + 1]
+    mine = jnp.int32(0)
+    for at in range(count):
+        mine = mine + pattern_smem[at % blocks, at // blocks]
+
+    pattern_out[...] = jnp.zeros_like(pattern_out)
+    pattern_out[0:blocks, 0:tiles] = pattern_vmem[...]
+
+    tile_of = lax.broadcasted_iota(jnp.int32, (ORBITALS, SPAN), 1) // BAS_TILE
+    named = supports_ref[...]
+    supported = (
+        (tile_of == named[:, 0:1]) | (tile_of == named[:, 1:2]) | (tile_of == named[:, 2:3])
+    )
+    orbitals = jnp.where(supported, coefficients_ref[...].astype(jnp.float32), 0.0)
+    weights[...] = jnp.zeros_like(weights)
+    weights[0:ORBITALS, 0:SPAN] = orbitals.astype(jnp.bfloat16)
+    weights[ORBITALS : 2 * ORBITALS, SPAN : 2 * SPAN] = orbitals.astype(jnp.bfloat16)
+
+    pl.semaphore_wait(barrier, n_bas + n_aux - 2)
+
+    pattern_copies = []
+    for k in range(1, n_bas):
+        pattern_copies.append(
+            pltpu.make_async_remote_copy(
+                src_ref=pattern_out,
+                dst_ref=pattern_in.at[me],
+                send_sem=pattern_send.at[k],
+                recv_sem=pattern_recv.at[k],
+                device_id={"bas": lax.rem(me + k, n_bas)},
+                device_id_type=MESH,
+            )
+        )
+        pattern_copies[-1].start()
+
+    for copy in loads:
+        copy.wait()
+
+    def transform(s, share):
+        at = listed[s]
+        tile = at // blocks
+        block = at - tile * blocks
+        width = AUX_TILE // n_bas
+        part = loaded[tile, pl.ds(share * width, width), block]
+        part = part.reshape(width // 2, 2, BAS_TILE, SPAN)
+        left = jnp.concatenate(
+            [part[:, 0].reshape(rows, SPAN), part[:, 1].reshape(rows, SPAN)], axis=1
+        )
+        return lax.dot_general(
+            left, weights[...], (((1,), (1,)), ((), ())), preferred_element_type=jnp.float32
+        ).astype(jnp.bfloat16)
+
+    copies = []
+    hand = None
+    first = 0
+    for stage, size in enumerate(STAGES):
+        if first + size > CAP - SPARE and hand is not None:
+            hand.wait()
+            hand = None
+
+        def fill(s, carry, mixed=first + size > CAP - SPARE):
+            for share in range(n_bas):
+                value = transform(s, share)
+                if mixed:
+                    other = spare_in[CAP - 1 - s, share]
+                    value = jnp.where(s < mine, value, other)
+                send_buf[share, s] = value
+            return carry
+
+        lax.fori_loop(first, first + size, fill, 0)
+        for k in range(1, n_bas):
+            peer = lax.rem(me + k, n_bas)
+            copies.append(
+                pltpu.make_async_remote_copy(
+                    src_ref=send_buf.at[peer, pl.ds(first, size)],
+                    dst_ref=recv_buf.at[me, pl.ds(first, size)],
+                    send_sem=send_sem.at[stage, k],
+                    recv_sem=recv_sem.at[stage, k],
+                    device_id={"bas": peer},
+                    device_id_type=MESH,
+                )
+            )
+            copies[-1].start()
+        if stage == HANDOVER_AFTER:
+
+            def spare(e, carry):
+                for share in range(n_bas):
+                    spare_out[e, share] = transform(CAP + e, share)
+                return carry
+
+            lax.fori_loop(0, SPARE, spare, 0)
+            hand = pltpu.make_async_remote_copy(
+                src_ref=spare_out,
+                dst_ref=spare_in,
+                send_sem=spare_send,
+                recv_sem=spare_recv,
+                device_id={"bas": sibling},
+                device_id_type=MESH,
+            )
+            hand.start()
+        first += size
+    own = pltpu.make_async_copy(send_buf.at[me], recv_buf.at[me, pl.ds(0, CAP)], own_sem)
+    own.start()
+
+    recv_buf[0, CAP] = jnp.zeros(recv_buf.shape[2:], recv_buf.dtype)
+    for copy in pattern_copies:
+        copy.wait()
+    pattern_in[me] = pattern_out[...]
+    local = pltpu.make_async_copy(pattern_in, pattern_all, pattern_local)
+    local.start()
+    local.wait()
+
+    def tally(q, counts):
+        return tuple(
+            counts[d] + sum(pattern_all[d, b, q] for b in range(blocks)) for d in range(n_bas)
+        )
+
+    counts = lax.fori_loop(0, tiles, tally, (jnp.int32(0),) * n_bas)
+    over = jnp.int32(0)
+    for d in range(0, n_bas, 2):
+        over = jnp.where(counts[d] + counts[d + 1] > 2 * CAP, 1, over)
+    for d in range(n_bas):
+        over = jnp.where(counts[d] > CAP + SPARE, 1, over)
+
+    own.wait()
+    for copy in copies:
+        copy.wait()
+
+    span_rows = n_bas * blocks * BAS_TILE
+    aux_rows = span_rows // n_aux
+    for a in range(n_aux):
+        partial[a, 0:aux_rows] = jnp.zeros((aux_rows, span_rows), jnp.float32)
+        partial[a, aux_rows:] = jnp.full(
+            (partial.shape[1] - aux_rows, span_rows), over, jnp.int32
+        ).astype(jnp.float32)
+
+    def gram(q, ranks):
+        ranks = list(ranks)
+        for d in range(n_bas):
+            for b in range(blocks):
+                here = pattern_all[d, b, q]
+                rank = ranks[d]
+                handed = rank >= CAP
+                source = jnp.where(handed, d + 1 - 2 * (d % 2), d)
+                slot = jnp.where(handed, jnp.maximum(2 * CAP - 1 - rank, 0), rank)
+                source = jnp.where(here > 0, source, 0)
+                slot = jnp.where(here > 0, slot, CAP)
+                value = recv_buf[source, slot]
+                top = (d * blocks + b) * BAS_TILE
+                for u in range(rows // BAS_TILE):
+                    dense[top : top + BAS_TILE, u * 128 : (u + 1) * 128] = value[
+                        u * BAS_TILE : (u + 1) * BAS_TILE
+                    ]
+                ranks[d] = rank + here
+        product = lax.dot_general(
+            dense[...], dense[...], (((1,), (1,)), ((), ())), preferred_element_type=jnp.float32
+        )
+        for a in range(n_aux):
+            partial[a, 0:aux_rows] += product[a * aux_rows : (a + 1) * aux_rows]
+        return tuple(ranks)
+
+    lax.fori_loop(0, tiles, gram, (jnp.int32(0),) * n_bas)
+
+    copies = []
+    for k in range(1, n_aux):
+        peer = lax.rem(my_aux + k, n_aux)
+        copies.append(
+            pltpu.make_async_remote_copy(
+                src_ref=partial.at[peer],
+                dst_ref=partial_in.at[my_aux],
+                send_sem=aux_send.at[k],
+                recv_sem=aux_recv.at[k],
+                device_id={"aux": peer},
+                device_id_type=MESH,
+            )
+        )
+        copies[-1].start()
+    partial_in[my_aux] = partial[my_aux]
+    for copy in copies:
+        copy.wait()
+    total = partial_in[0]
+    for a in range(1, n_aux):
+        total = total + partial_in[a]
+    flag_ref[...] = total[aux_rows:, 0:128]
+
+    own_rows = aux_rows // n_bas
+    for d in range(n_bas):
+        summed[d, 0:own_rows] = total[d * own_rows : (d + 1) * own_rows]
+    copies = []
+    for k in range(1, n_bas):
+        peer = lax.rem(me + k, n_bas)
+        copies.append(
+            pltpu.make_async_remote_copy(
+                src_ref=summed.at[peer],
+                dst_ref=summed_in.at[me],
+                send_sem=bas_send.at[k],
+                recv_sem=bas_recv.at[k],
+                device_id={"bas": peer},
+                device_id_type=MESH,
+            )
+        )
+        copies[-1].start()
+    summed_in[me] = summed[me]
+    for copy in copies:
+        copy.wait()
+    total = summed_in[0]
+    for d in range(1, n_bas):
+        total = total + summed_in[d]
+    out_ref[...] = total[0:own_rows]
+
+
+def body(n_aux, n_bas, integrals, coefficients, supports, tile_pattern):
+    tiles, blocks = tile_pattern.shape
+    window = n_bas * blocks * BAS_TILE
+    rows = AUX_TILE // n_bas // 2 * BAS_TILE
+    aux_rows = window // n_aux
+    own_rows = aux_rows // n_bas
+    vmem = pl.BlockSpec(memory_space=pltpu.VMEM)
+    dma = pltpu.SemaphoreType.DMA
+    bf16, f32, i32 = jnp.bfloat16, jnp.float32, jnp.int32
+    result, flag = pl.pallas_call(
+        functools.partial(kernel, n_aux, n_bas, tiles, blocks),
+        out_shape=(
+            jax.ShapeDtypeStruct((own_rows, window), f32),
+            jax.ShapeDtypeStruct((8, 128), f32),
+        ),
+        in_specs=[
+            pl.BlockSpec(memory_space=pltpu.SMEM),
+            vmem,
+            vmem,
+            vmem,
+            pl.BlockSpec(memory_space=pl.ANY),
+        ],
+        out_specs=(vmem, vmem),
+        scratch_shapes=[
+            pltpu.VMEM((tiles, AUX_TILE, blocks, BAS_TILE, SPAN), bf16),
+            pltpu.VMEM((2 * ORBITALS, 2 * SPAN), bf16),
+            pltpu.VMEM((n_bas, CAP, rows, 2 * ORBITALS), bf16),
+            pltpu.VMEM((n_bas, CAP + 1, rows, 2 * ORBITALS), bf16),
+            pltpu.VMEM((SPARE, n_bas, rows, 2 * ORBITALS), bf16),
+            pltpu.VMEM((SPARE, n_bas, rows, 2 * ORBITALS), bf16),
+            pltpu.VMEM((window, rows // BAS_TILE * 2 * ORBITALS), bf16),
+            pltpu.VMEM((n_aux, aux_rows + 8, window), f32),
+            pltpu.VMEM((n_aux, aux_rows + 8, window), f32),
+            pltpu.VMEM((n_bas, 8, window), f32),
+            pltpu.VMEM((n_bas, 8, window), f32),
+            pltpu.VMEM((8, 128), i32),
+            pltpu.VMEM((n_bas, 8, 128), i32),
+            pltpu.SMEM((n_bas, 8, 128), i32),
+            pltpu.SMEM((tiles * blocks + 1,), i32),
+            pltpu.SMEM((CAP + SPARE,), i32),
+            dma((tiles,)),
+            dma((n_bas,)),
+            dma((n_bas,)),
+            dma,
+            dma((len(STAGES), n_bas)),
+            dma((len(STAGES), n_bas)),
+            dma,
+            dma,
+            dma,
+            dma((n_aux,)),
+            dma((n_aux,)),
+            dma((n_bas,)),
+            dma((n_bas,)),
+        ],
+        compiler_params=pltpu.CompilerParams(
+            collective_id=0, has_side_effects=True, vmem_limit_bytes=60 * 2**20
+        ),
+        name="exchange",
+    )(
+        tile_pattern.T,
+        tile_pattern.T,
+        supports,
+        coefficients.T,
+        integrals.reshape(tiles, AUX_TILE, blocks, BAS_TILE, SPAN),
+    )
+    return lax.cond(
+        flag[0, 0] > 0.0,
+        lambda: dense_body(integrals, coefficients, supports, tile_pattern),
+        lambda: result,
+    )
+
+
 def solution(mesh):
     in_specs = (P("aux", "bas", None), P(), P(), P("aux", "bas"))
     out_specs = P(("aux", "bas"), None)
-    return jax.shard_map(body, mesh=mesh, in_specs=in_specs, out_specs=out_specs, check_vma=False)
+    return jax.shard_map(
+        functools.partial(body, mesh.shape["aux"], mesh.shape["bas"]),
+        mesh=mesh,
+        in_specs=in_specs,
+        out_specs=out_specs,
+        check_vma=False,
+    )

time: 432 us -> 148 us (0.34)
  waiting for transfers between devices: 146 us -> 0 us
  blocking collectives: 138 us -> 0 us
  Pallas kernels: 0 us -> 131 us
  local copies, waits for them, and re-layouts: 92.5 us -> 3.17 us
  matrix products: 38.6 us -> 0 us
    unnamed x2 -> x0, waiting for transfers between devices: 146 us -> none
    all_to_all x1 -> x0, blocking collectives: 138 us -> none  [body(): lax.all_to_all(transformed, 'bas', split_axis=1, concat_axis=2, tiled=True)]
    pallas_call x0 -> x1, Pallas kernels: none -> 131 us  [body(): pl.pallas_call(functools.partial(kernel, n_aux, n_bas, tiles, blocks), ou...]
    all_to_all x1 -> x0, local copies, waits for them, and re-layouts: 41.9 us -> none  [body(): lax.all_to_all(transformed, 'bas', split_axis=1, concat_axis=2, tiled=True)]
    reshape x1 -> x0, local copies, waits for them, and re-layouts: 40 us -> none  [body(): stacked = redistributed.reshape(-1, window_rows)]
    dot_general x2 -> x0, matrix products: 38.6 us -> none  [the longest x1 23.6 us: body(): jnp.einsum('pmn,ni->pim', integrals, orbitals, preferred_element_type=jnp...]
    convert_element_type x1 -> x0, local copies, waits for them, and re-layouts: 9.01 us -> none  [body(): transformed = (transformed * screening[:, None, :]).astype(jnp.bfloat16)]
  transfers between devices with their start and end apart: 1 -> 0, of which waited for: 1 -> 0; matrix products, arithmetic and copies ran while one was open for 0% -> 0% of each run, Pallas kernels for 0% -> 0%
where the time goes in v1:
time: 148 us
  Pallas kernels  131 us (89%)
  between operations  14.1 us (10%)
  local copies, waits for them, and re-layouts  3.17 us (2%)
    pallas_call x1, Pallas kernels, body(): pl.pallas_call(functools.partial(kernel, n_aux, n_bas, tiles, blocks), ou...  131 us

profile of v1, /device:TPU:1, one launch (start us, length us, event | category | flops | bytes accessed | tf_op | source)
XLA Modules:
  0.0 148.1 jit_solution(15603955625862914947)
XLA Ops:
  6.5 1.4 copy.21.supports_ref
  7.9 0.0 copy-start
  7.9 0.0 copy-start.1
  7.9 0.0 copy-start.2
  7.9 130.7 %exchange.1 = (f32[3,384]{1,0:T(4,128)S(1)}, f32[8,128]{1,0:T(8,128)}) custom-call(s32[3,15]{1,0:T(4,128)} %bitcast.29, s32[3,15]{1,0:T(4,128)} %bitcast.30, s32[64,3]{1,0:T(8,128)} %copy.21.supports_ref, bf16[64,128]{1,0:T(8,128)(2,1)} %bitcast.28, bf16[15,128,3,16,128]{4,3,2,1,0:T(8,128)(2,1)} %bitcast.23), custom_call_target="tpu_custom_call" | custom-call | tf_op jit(solution)/shard_map/exchange/pallas_call | solution.py:336
  138.6 1.2 slice.3
  140.4 0.0 copy-done
  140.4 0.0 copy-done.1
  140.5 0.0 copy-done.2
  140.5 0.2 conditional.1
  140.7 0.6 copy.34
Async XLA Ops:
  7.9 132.5 %copy-start = (bf16[128,64]{0,1:T(8,128)(2,1)S(1)}, bf16[128,64]{0,1:T(8,128)(2,1)}, u32[]{:S(2)}) copy-start(bf16[128,64]{0,1:T(8,128)(2,1)} %param.7) | copy-start | bytes 49156
  7.9 132.5 %copy-start.1 = (s32[15,3]{0,1:T(4,128)S(1)}, s32[15,3]{0,1:T(4,128)}, u32[]{:S(2)}) copy-start(s32[15,3]{0,1:T(4,128)} %param.9) | copy-start | bytes 544
  7.9 132.6 %copy-start.2 = (s32[64,3]{0,1:T(4,128)S(1)}, s32[64,3]{0,1:T(4,128)}, u32[]{:S(2)}) copy-start(s32[64,3]{0,1:T(4,128)} %param.8) | copy-start | bytes 2308

commit v2 on v1

v2 whole, which is shorter than its diff:
```python
import functools

import jax
import jax.numpy as jnp
from jax import lax
from jax.experimental import pallas as pl
from jax.experimental.pallas import tpu as pltpu
from jax.sharding import PartitionSpec as P

AUX_TILE = 128
BAS_TILE = 16
ORBITALS = 64
SPAN = 128
MESH = pl.DeviceIdType.MESH

CAP = 31
SPARE = 8
STAGES = (3, 4, 4, 4, 4, 4, 4, 4)
HANDOVER_AFTER = 1
HEAD = 3
HEAD_TILES = 4
EARLY_TILES = 9
EARLY = 27
GROUP = 3


def dense_body(integrals, coefficients, supports, tile_pattern):
    span = integrals.shape[2]
    tile_of = jnp.arange(span) // BAS_TILE
    supported = jnp.any(tile_of[:, None, None] == supports[None, :, :], axis=2)
    orbitals = jnp.where(supported, coefficients, jnp.zeros_like(coefficients))
    screening = jnp.repeat(jnp.repeat(tile_pattern, BAS_TILE, axis=1), AUX_TILE, axis=0).astype(
        jnp.float32
    )
    transformed = jnp.einsum("pmn,ni->pim", integrals, orbitals, preferred_element_type=jnp.float32)
    transformed = (transformed * screening[:, None, :]).astype(jnp.bfloat16)
    contract = (((0,), (0,)), ((), ()))
    redistributed = lax.all_to_all(transformed, "bas", split_axis=1, concat_axis=2, tiled=True)
    window_rows = redistributed.shape[2]
    stacked = redistributed.reshape(-1, window_rows)
    total = lax.dot_general(stacked, stacked, contract, preferred_element_type=jnp.float32)
    for axis in ("aux", "bas"):
        total = total.reshape(lax.axis_size(axis), -1, window_rows)
        total = jnp.sum(lax.all_to_all(total, axis, split_axis=0, concat_axis=0), axis=0)
    return total


def kernel(
    n_aux,
    n_bas,
    tiles,
    blocks,
    pattern_smem,
    pattern_vmem,
    supports_ref,
    coefficients_ref,
    integrals_ref,
    out_ref,
    flag_ref,
    loaded_head,
    loaded,
    weights,
    send_buf,
    recv_early,
    recv_late,
    spare_out,
    spare_in,
    dense,
    wide,
    corner,
    partial,
    pair_in,
    half,
    partial_in,
    summed,
    summed_in,
    pattern_out,
    pattern_in,
    pattern_all,
    flag_out,
    flag_in,
    flag_smem,
    following,
    listed,
    head_sem,
    load_sem,
    pattern_send,
    pattern_recv,
    pattern_local,
    send_sem,
    recv_sem,
    own_sem,
    spare_send,
    spare_recv,
    flag_send,
    flag_recv,
    flag_local,
    pair_send,
    pair_recv,
    aux_send,
    aux_recv,
    bas_send,
    bas_recv,
):
    my_aux = lax.axis_index("aux")
    me = lax.axis_index("bas")
    sibling = me + 1 - 2 * lax.rem(me, 2)
    count = tiles * blocks
    rows = AUX_TILE // n_bas // 2 * BAS_TILE

    head = pltpu.make_async_copy(integrals_ref.at[pl.ds(0, HEAD_TILES)], loaded_head, head_sem)
    head.start()
    loads = []
    for q in range(HEAD_TILES, tiles):
        loads.append(
            pltpu.make_async_copy(integrals_ref.at[q], loaded.at[q], load_sem.at[q])
        )
        loads[-1].start()

    barrier = pltpu.get_barrier_semaphore()
    for k in range(1, n_bas):
        pl.semaphore_signal(
            barrier, inc=1, device_id={"bas": lax.rem(me + k, n_bas)}, device_id_type=MESH
        )
    for k in range(1, n_aux):
        pl.semaphore_signal(
            barrier, inc=1, device_id={"aux": lax.rem(my_aux + k, n_aux)}, device_id_type=MESH
        )

    following[count] = jnp.int32(count - 1)
    upcoming = jnp.int32(count - 1)
    for at in reversed(range(count)):
        upcoming = jnp.where(pattern_smem[at % blocks, at // blocks] > 0, at, upcoming)
        following[at] = upcoming
    mine = jnp.int32(0)
    for at in range(count):
        if at == HEAD_TILES * blocks:
            short = mine < HEAD
            mine = jnp.maximum(mine, HEAD)
        mine = mine + pattern_smem[at % blocks, at // blocks]
    at = following[0]
    for s in range(CAP + SPARE):
        if s == HEAD:
            at = jnp.where(short, following[HEAD_TILES * blocks], at)
        listed[s] = at
        at = following[at + 1]

    pattern_out[...] = jnp.zeros_like(pattern_out)
    pattern_out[0:blocks, 0:tiles] = pattern_vmem[...]

    tile_of = lax.broadcasted_iota(jnp.int32, (SPAN, ORBITALS), 0) // BAS_TILE
    named = supports_ref[...]
    supported = tile_of == named[0:1]
    for k in range(1, named.shape[0]):
        supported = supported | (tile_of == named[k : k + 1])
    diagonal = lax.broadcasted_iota(jnp.int32, (ORBITALS, ORBITALS), 0) == (
        lax.broadcasted_iota(jnp.int32, (ORBITALS, ORBITALS), 1)
    )
    turned = lax.dot_general(
        jnp.where(diagonal, 1.0, 0.0).astype(jnp.bfloat16),
        jnp.where(supported, 1.0, 0.0).astype(jnp.bfloat16),
        (((1,), (1,)), ((), ())),
        preferred_element_type=jnp.float32,
    )
    orbitals = jnp.where(turned > 0.5, coefficients_ref[...].astype(jnp.float32), 0.0)
    weights[...] = jnp.zeros_like(weights)
    weights[0:ORBITALS, 0:SPAN] = orbitals.astype(jnp.bfloat16)
    weights[ORBITALS : 2 * ORBITALS, SPAN : 2 * SPAN] = orbitals.astype(jnp.bfloat16)

    head.wait()
    loads.append(pltpu.make_async_copy(loaded_head, loaded.at[pl.ds(0, HEAD_TILES)], head_sem))
    loads[-1].start()

    def transform(s, share, source, limit):
        at = jnp.minimum(listed[s], limit * blocks - 1)
        tile = at // blocks
        block = at - tile * blocks
        width = AUX_TILE // n_bas
        part = source[tile, pl.ds(share * width, width), block]
        part = part.reshape(width // 2, 2, BAS_TILE, SPAN)
        left = jnp.concatenate(
            [part[:, 0].reshape(rows, SPAN), part[:, 1].reshape(rows, SPAN)], axis=1
        )
        return lax.dot_general(
            left, weights[...], (((1,), (1,)), ((), ())), preferred_element_type=jnp.float32
        ).astype(jnp.bfloat16)

    copies = []
    hand = None
    first = 0
    for stage, size in enumerate(STAGES):
        if first + size > CAP - SPARE and hand is not None:
            hand.wait()
            hand = None

        if first == HEAD:
            for copy in loads:
                copy.wait()
        source, limit = (loaded_head, HEAD_TILES) if first < HEAD else (loaded, tiles)

        def fill(s, carry, mixed=first + size > CAP - SPARE, source=source, limit=limit):
            for share in range(n_bas):
                value = transform(s, share, source, limit)
                if mixed:
                    other = spare_in[CAP - 1 - s, share]
                    value = jnp.where(s < mine, value, other)
                send_buf[share, s] = value
            return carry

        lax.fori_loop(first, first + size, fill, 0)
        if stage == 0:
            pl.semaphore_wait(barrier, n_bas + n_aux - 2)

            pattern_copies = []
            for k in range(1, n_bas):
                pattern_copies.append(
                    pltpu.make_async_remote_copy(
                        src_ref=pattern_out,
                        dst_ref=pattern_in.at[me],
                        send_sem=pattern_send.at[k],
                        recv_sem=pattern_recv.at[k],
                        device_id={"bas": lax.rem(me + k, n_bas)},
                        device_id_type=MESH,
                    )
                )
                pattern_copies[-1].start()
        for k in range(1, n_bas):
            peer = lax.rem(me + k, n_bas)
            where = (recv_early, first) if first < EARLY else (recv_late, first - EARLY)
            copies.append(
                pltpu.make_async_remote_copy(
                    src_ref=send_buf.at[peer, pl.ds(first, size)],
                    dst_ref=where[0].at[me, pl.ds(where[1], size)],
                    send_sem=send_sem.at[stage, k],
                    recv_sem=recv_sem.at[stage, k],
                    device_id={"bas": peer},
                    device_id_type=MESH,
                )
            )
            copies[-1].start()
        if stage == HANDOVER_AFTER:

            def spare(e, carry):
                for share in range(n_bas):
                    spare_out[e, share] = transform(CAP + e, share, loaded, tiles)
                return carry

            lax.fori_loop(0, SPARE, spare, 0)
            hand = pltpu.make_async_remote_copy(
                src_ref=spare_out,
                dst_ref=spare_in,
                send_sem=spare_send,
                recv_sem=spare_recv,
                device_id={"bas": sibling},
                device_id_type=MESH,
            )
            hand.start()
        first += size
    owns = [
        pltpu.make_async_copy(
            send_buf.at[me, pl.ds(0, EARLY)], recv_early.at[me, pl.ds(0, EARLY)], own_sem.at[0]
        ),
        pltpu.make_async_copy(
            send_buf.at[me, pl.ds(EARLY, CAP - EARLY)],
            recv_late.at[me, pl.ds(0, CAP - EARLY)],
            own_sem.at[1],
        ),
    ]
    for copy in owns:
        copy.start()

    recv_early[0, EARLY] = jnp.zeros(recv_early.shape[2:], recv_early.dtype)
    for copy in pattern_copies:
        copy.wait()
    pattern_in[me] = pattern_out[...]
    local = pltpu.make_async_copy(pattern_in, pattern_all, pattern_local)
    local.start()
    local.wait()

    def tally(q, counts):
        return tuple(
            jnp.where(q == HEAD_TILES, jnp.maximum(counts[d], HEAD), counts[d])
            + sum(pattern_all[d, b, q] for b in range(blocks))
            for d in range(n_bas)
        )

    counts = lax.fori_loop(0, tiles, tally, (jnp.int32(0),) * n_bas)
    over = jnp.int32(0)
    for d in range(0, n_bas, 2):
        over = jnp.where(counts[d] + counts[d + 1] > 2 * CAP, 1, over)
    for d in range(n_bas):
        over = jnp.where(counts[d] > CAP + SPARE, 1, over)
    flag_out[...] = jnp.full(flag_out.shape, over, jnp.int32)
    flag_copies = []
    for k in range(1, n_aux):
        flag_copies.append(
            pltpu.make_async_remote_copy(
                src_ref=flag_out,
                dst_ref=flag_in.at[my_aux],
                send_sem=flag_send.at[k],
                recv_sem=flag_recv.at[k],
                device_id={"aux": lax.rem(my_aux + k, n_aux)},
                device_id_type=MESH,
            )
        )
        flag_copies[-1].start()
    flag_in[my_aux] = flag_out[...]

    span_rows = n_bas * blocks * BAS_TILE
    aux_rows = span_rows // n_aux
    square = wide.shape[1]
    depth = rows // BAS_TILE * 128
    wide[...] = jnp.zeros_like(wide)
    corner[...] = jnp.zeros_like(corner)

    def gram(group, ranks, late):
        ranks = list(ranks)
        for step in range(GROUP):
            q = group * GROUP + step
            for d in range(n_bas):
                ranks[d] = jnp.where(q == HEAD_TILES, jnp.maximum(ranks[d], HEAD), ranks[d])
                for b in range(blocks):
                    here = pattern_all[d, b, q] > 0
                    rank = ranks[d]
                    if late:
                        handed = rank >= CAP
                        source = jnp.where(handed, d + 1 - 2 * (d % 2), d)
                        slot = jnp.where(handed, jnp.maximum(2 * CAP - 1 - rank, 0), rank)
                        last = here & (slot >= EARLY)
                        first = here & (slot < EARLY)
                        value = jnp.where(
                            last,
                            recv_late[source, jnp.clip(slot - EARLY, 0, CAP - EARLY - 1)],
                            recv_early[jnp.where(first, source, 0), jnp.where(first, slot, EARLY)],
                        )
                    else:
                        value = recv_early[jnp.where(here, d, 0), jnp.where(here, rank, EARLY)]
                    top = (d * blocks + b) * BAS_TILE
                    for u in range(rows // BAS_TILE):
                        at = step * depth + u * 128
                        dense[top : top + BAS_TILE, at : at + 128] = value[
                            u * BAS_TILE : (u + 1) * BAS_TILE
                        ]
                    ranks[d] = rank + pattern_all[d, b, q]
        contract = (((1,), (1,)), ((), ()))
        wide[...] += lax.dot_general(
            dense[...], dense[0:square], contract, preferred_element_type=jnp.float32
        )
        corner[...] += lax.dot_general(
            dense[square:], dense[square:], contract, preferred_element_type=jnp.float32
        )
        return tuple(ranks)

    first = 0
    ranks = (jnp.int32(0),) * n_bas
    for stage, size in enumerate(STAGES):
        if first == EARLY:
            owns[0].wait()
            ranks = lax.fori_loop(
                0, EARLY_TILES // GROUP, functools.partial(gram, late=False), ranks
            )
        for copy in copies[stage * (n_bas - 1) : (stage + 1) * (n_bas - 1)]:
            copy.wait()
        first += size
    owns[1].wait()
    lax.fori_loop(
        EARLY_TILES // GROUP, tiles // GROUP, functools.partial(gram, late=True), ranks
    )
    for a in range(n_aux):
        low, high = a * aux_rows, (a + 1) * aux_rows
        partial[a, :, 0:square] = wide[low:high]
        if low >= square:
            partial[a, :, square:] = corner[low - square : high - square]
    own_rows = aux_rows // n_bas
    turned = wide[square:].T
    for a in range(n_aux):
        low, high = a * aux_rows, min((a + 1) * aux_rows, square)
        if low < square:
            partial[a, 0 : high - low, square:] = turned[low:high]
            if high < low + aux_rows:
                partial[a, high - low :, square:] = corner[0 : low + aux_rows - high]

    core = lax.rem(me, 2)
    n_half = n_aux // 2
    pair = pltpu.make_async_remote_copy(
        src_ref=partial.at[pl.ds((1 - core) * n_half, n_half)],
        dst_ref=pair_in,
        send_sem=pair_send,
        recv_sem=pair_recv,
        device_id={"bas": sibling},
        device_id_type=MESH,
    )
    pair.start()
    pair.wait()
    for i in range(n_half):
        half[i] = partial[core * n_half + i] + pair_in[i]

    keeps = my_aux // n_half == core
    other = jnp.where(keeps, 0, 1)
    copies = []
    for k in range(n_half):
        place = lax.rem(my_aux + k, n_half)
        copies.append(
            pltpu.make_async_remote_copy(
                src_ref=half.at[place],
                dst_ref=partial_in.at[my_aux],
                send_sem=aux_send.at[k],
                recv_sem=aux_recv.at[k + n_half * other],
                device_id={"aux": core * n_half + place},
                device_id_type=MESH,
            )
        )
    for k in range(1, n_half):
        copies[k].start()

    @pl.when(jnp.logical_not(keeps))
    def _():
        copies[0].start()
        for copy in copies:
            copy.wait_send()

    @pl.when(keeps)
    def _():
        partial_in[my_aux] = half[lax.rem(my_aux, n_half)]
        for k in range(1, n_aux):
            pltpu.make_async_remote_copy(
                src_ref=half.at[0],
                dst_ref=partial_in.at[0],
                send_sem=aux_send.at[0],
                recv_sem=aux_recv.at[k],
                device_id={"aux": my_aux},
                device_id_type=MESH,
            ).wait_recv()
        for k in range(1, n_half):
            copies[k].wait_send()
        total = partial_in[0]
        for a in range(1, n_aux):
            total = total + partial_in[a]
        for d in range(n_bas):
            summed[d, 0:own_rows] = total[d * own_rows : (d + 1) * own_rows]
        summed_in[me] = summed[me]

    copies = []
    for k in range(1, n_bas):
        peer = lax.rem(me + k, n_bas)
        copies.append(
            pltpu.make_async_remote_copy(
                src_ref=summed.at[peer],
                dst_ref=summed_in.at[me],
                send_sem=bas_send.at[k],
                recv_sem=bas_recv.at[k],
                device_id={"bas": peer},
                device_id_type=MESH,
            )
        )

    @pl.when(keeps)
    def _():
        for copy in copies:
            copy.start()

    giver = my_aux // n_half
    for k in range(1, n_bas):

        @pl.when(lax.rem(me + n_bas - k, 2) == giver)
        def _(k=k):
            copies[k - 1].wait_recv()

    total = summed_in[giver]
    for d in range(2, n_bas, 2):
        total = total + summed_in[giver + d]
    out_ref[...] = total[0:own_rows]

    @pl.when(keeps)
    def _():
        for copy in copies:
            copy.wait_send()

    for copy in flag_copies:
        copy.wait()
    flagged = flag_in[0]
    for a in range(1, n_aux):
        flagged = jnp.maximum(flagged, flag_in[a])
    flag_out[...] = flagged
    local = pltpu.make_async_copy(flag_out, flag_smem, flag_local)
    local.start()
    local.wait()
    flag_ref[0, 0] = flag_smem[0, 0]


def body(n_aux, n_bas, integrals, coefficients, supports, tile_pattern):
    tiles, blocks = tile_pattern.shape
    window = n_bas * blocks * BAS_TILE
    rows = AUX_TILE // n_bas // 2 * BAS_TILE
    aux_rows = window // n_aux
    own_rows = aux_rows // n_bas
    square = window // 3 * 2
    vmem = pl.BlockSpec(memory_space=pltpu.VMEM)
    dma = pltpu.SemaphoreType.DMA
    bf16, f32, i32 = jnp.bfloat16, jnp.float32, jnp.int32
    result, flag = pl.pallas_call(
        functools.partial(kernel, n_aux, n_bas, tiles, blocks),
        out_shape=(
            jax.ShapeDtypeStruct((own_rows, window), f32),
            jax.ShapeDtypeStruct((1, 1), i32),
        ),
        in_specs=[
            pl.BlockSpec(memory_space=pltpu.SMEM),
            vmem,
            vmem,
            vmem,
            pl.BlockSpec(memory_space=pl.ANY),
        ],
        out_specs=(vmem, pl.BlockSpec(memory_space=pltpu.SMEM)),
        scratch_shapes=[
            pltpu.VMEM((HEAD_TILES, AUX_TILE, blocks, BAS_TILE, SPAN), bf16),
            pltpu.VMEM((tiles, AUX_TILE, blocks, BAS_TILE, SPAN), bf16),
            pltpu.VMEM((2 * ORBITALS, 2 * SPAN), bf16),
            pltpu.VMEM((n_bas, CAP, rows, 2 * ORBITALS), bf16),
            pltpu.VMEM((n_bas, EARLY + 1, rows, 2 * ORBITALS), bf16),
            pltpu.VMEM((n_bas, CAP - EARLY, rows, 2 * ORBITALS), bf16),
            pltpu.VMEM((SPARE, n_bas, rows, 2 * ORBITALS), bf16),
            pltpu.VMEM((SPARE, n_bas, rows, 2 * ORBITALS), bf16),
            pltpu.VMEM((window, GROUP * rows // BAS_TILE * 2 * ORBITALS), bf16),
            pltpu.VMEM((window, square), f32),
            pltpu.VMEM((window - square, window - square), f32),
            pltpu.VMEM((n_aux, aux_rows, window), f32),
            pltpu.VMEM((n_aux // 2, aux_rows, window), f32),
            pltpu.VMEM((n_aux // 2, aux_rows, window), f32),
            pltpu.VMEM((n_aux, aux_rows, window), f32),
            pltpu.VMEM((n_bas, 8, window), f32),
            pltpu.VMEM((n_bas, 8, window), f32),
            pltpu.VMEM((8, 128), i32),
            pltpu.VMEM((n_bas, 8, 128), i32),
            pltpu.SMEM((n_bas, 8, 128), i32),
            pltpu.VMEM((8, 128), i32),
            pltpu.VMEM((n_aux, 8, 128), i32),
            pltpu.SMEM((8, 128), i32),
            pltpu.SMEM((tiles * blocks + 1,), i32),
            pltpu.SMEM((CAP + SPARE,), i32),
            dma,
            dma((tiles,)),
            dma((n_bas,)),
            dma((n_bas,)),
            dma,
            dma((len(STAGES), n_bas)),
            dma((len(STAGES), n_bas)),
            dma((2,)),
            dma,
            dma,
            dma((n_aux,)),
            dma((n_aux,)),
            dma,
            dma,
            dma,
            dma((n_aux,)),
            dma((n_aux,)),
            dma((n_bas,)),
            dma((n_bas,)),
        ],
        compiler_params=pltpu.CompilerParams(
            collective_id=0, has_side_effects=True, vmem_limit_bytes=60 * 2**20
        ),
        name="exchange",
    )(
        tile_pattern.T,
        tile_pattern.T,
        supports.T,
        coefficients.T,
        integrals.reshape(tiles, AUX_TILE, blocks, BAS_TILE, SPAN),
    )
    return lax.cond(
        flag[0, 0] > 0,
        lambda: dense_body(integrals, coefficients, supports, tile_pattern),
        lambda: result,
    )


def solution(mesh):
    in_specs = (P("aux", "bas", None), P(), P(), P("aux", "bas"))
    out_specs = P(("aux", "bas"), None)
    return jax.shard_map(
        functools.partial(body, mesh.shape["aux"], mesh.shape["bas"]),
        mesh=mesh,
        in_specs=in_specs,
        out_specs=out_specs,
        check_vma=False,
    )
```

time: 148 us -> 125 us (0.84)
  between operations: 14.1 us -> 0.74 us
  Pallas kernels: 131 us -> 123 us
  local copies, waits for them, and re-layouts: 3.17 us -> 0.61 us
    pallas_call x1, Pallas kernels: 131 us -> 123 us  [body(): pl.pallas_call(functools.partial(kernel, n_aux, n_bas, tiles, blocks), ou...]
where the time goes in v2:
time: 125 us; the launch traced here: 124 us
  Pallas kernels  123 us (98%)
    pallas_call x1, Pallas kernels, body(): pl.pallas_call(functools.partial(kernel, n_aux, n_bas, tiles, blocks), ou...  123 us

profile of v2, /device:TPU:1, one launch (start us, length us, event | category | flops | bytes accessed | tf_op | source)
XLA Modules:
  0.0 124.3 jit_solution(9654490622004517065)
XLA Ops:
  0.0 0.0 copy-start
  0.0 0.0 copy-start.1
  0.0 0.0 copy-start.2
  0.0 122.8 %exchange.1 = (f32[3,384]{1,0:T(4,128)S(1)}, s32[1,1]{1,0:T(1,128)}) custom-call(s32[3,15]{1,0:T(4,128)} %bitcast.37, s32[3,15]{1,0:T(4,128)} %bitcast.38, s32[3,64]{1,0:T(4,128)} %bitcast.39, bf16[64,128]{1,0:T(8,128)(2,1)} %bitcast.36, bf16[15,128,3,16,128]{4,3,2,1,0:T(8,128)(2,1)} %bitcast.29), custom_call_target="tpu_custom_call" | custom-call | tf_op jit(solution)/shard_map/exchange/pallas_call | solution.py:501
  123.5 0.0 copy-done
  123.5 0.0 copy-done.1
  123.5 0.0 copy-done.2
  123.5 0.2 conditional.1
  123.8 0.6 copy.34
Async XLA Ops:
  0.0 123.5 %copy-start = (bf16[128,64]{0,1:T(8,128)(2,1)S(1)}, bf16[128,64]{0,1:T(8,128)(2,1)}, u32[]{:S(2)}) copy-start(bf16[128,64]{0,1:T(8,128)(2,1)} %param.7) | copy-start | bytes 49156
  0.0 123.5 %copy-start.1 = (s32[15,3]{0,1:T(4,128)S(1)}, s32[15,3]{0,1:T(4,128)}, u32[]{:S(2)}) copy-start(s32[15,3]{0,1:T(4,128)} %param.9) | copy-start | bytes 544
  0.0 123.5 %copy-start.2 = (s32[64,3]{0,1:T(4,128)S(1)}, s32[64,3]{0,1:T(4,128)}, u32[]{:S(2)}) copy-start(s32[64,3]{0,1:T(4,128)} %param.8) | copy-start | bytes 2308

commit v3 on v2

--- a/solution.py
+++ b/solution.py
@@ -115,7 +115,6 @@
         loads.append(
             pltpu.make_async_copy(integrals_ref.at[q], loaded.at[q], load_sem.at[q])
         )
-        loads[-1].start()
 
     barrier = pltpu.get_barrier_semaphore()
     for k in range(1, n_bas):
@@ -168,6 +167,8 @@
     weights[ORBITALS : 2 * ORBITALS, SPAN : 2 * SPAN] = orbitals.astype(jnp.bfloat16)
 
     head.wait()
+    for copy in loads:
+        copy.start()
     loads.append(pltpu.make_async_copy(loaded_head, loaded.at[pl.ds(0, HEAD_TILES)], head_sem))
     loads[-1].start()
 

time: 125 us -> 120 us (0.960)
  Pallas kernels: 123 us -> 118 us
    pallas_call x1, Pallas kernels: 123 us -> 118 us  [body(): pl.pallas_call(functools.partial(kernel, n_aux, n_bas, tiles, blocks), ou...]
where the time goes in v3:
time: 120 us
  Pallas kernels  118 us (98%)
    pallas_call x1, Pallas kernels, body(): pl.pallas_call(functools.partial(kernel, n_aux, n_bas, tiles, blocks), ou...  118 us

profile of v3, /device:TPU:1, one launch (start us, length us, event | category | flops | bytes accessed | tf_op | source)
XLA Modules:
  0.0 119.8 jit_solution(12304871306806171658)
XLA Ops:
  0.0 0.0 copy-start
  0.0 0.0 copy-start.1
  0.0 0.0 copy-start.2
  0.0 118.2 %exchange.1 = (f32[3,384]{1,0:T(4,128)S(1)}, s32[1,1]{1,0:T(1,128)}) custom-call(s32[3,15]{1,0:T(4,128)} %bitcast.37, s32[3,15]{1,0:T(4,128)} %bitcast.38, s32[3,64]{1,0:T(4,128)} %bitcast.39, bf16[64,128]{1,0:T(8,128)(2,1)} %bitcast.36, bf16[15,128,3,16,128]{4,3,2,1,0:T(8,128)(2,1)} %bitcast.29), custom_call_target="tpu_custom_call" | custom-call | tf_op jit(solution)/shard_map/exchange/pallas_call | solution.py:502
  118.9 0.0 copy-done
  118.9 0.0 copy-done.1
  118.9 0.0 copy-done.2
  118.9 0.2 conditional.1
  119.2 0.6 copy.34
Async XLA Ops:
  0.0 118.9 %copy-start = (bf16[128,64]{0,1:T(8,128)(2,1)S(1)}, bf16[128,64]{0,1:T(8,128)(2,1)}, u32[]{:S(2)}) copy-start(bf16[128,64]{0,1:T(8,128)(2,1)} %param.7) | copy-start | bytes 49156
  0.0 118.9 %copy-start.1 = (s32[15,3]{0,1:T(4,128)S(1)}, s32[15,3]{0,1:T(4,128)}, u32[]{:S(2)}) copy-start(s32[15,3]{0,1:T(4,128)} %param.9) | copy-start | bytes 544
  0.0 118.9 %copy-start.2 = (s32[64,3]{0,1:T(4,128)S(1)}, s32[64,3]{0,1:T(4,128)}, u32[]{:S(2)}) copy-start(s32[64,3]{0,1:T(4,128)} %param.8) | copy-start | bytes 2308

commit v4 on v3

--- a/solution.py
+++ b/solution.py
@@ -381,8 +381,17 @@
             if high < low + aux_rows:
                 partial[a, high - low :, square:] = corner[0 : low + aux_rows - high]
 
+    for copy in flag_copies:
+        copy.wait()
+    flagged = flag_in[0]
+    for a in range(1, n_aux):
+        flagged = jnp.maximum(flagged, flag_in[a])
+
     core = lax.rem(me, 2)
+    chip = me // 2
     n_half = n_aux // 2
+    n_chip = n_bas // 2
+    chip_rows = 2 * own_rows
     pair = pltpu.make_async_remote_copy(
         src_ref=partial.at[pl.ds((1 - core) * n_half, n_half)],
         dst_ref=pair_in,
@@ -394,94 +403,69 @@
     pair.start()
     pair.wait()
     for i in range(n_half):
-        half[i] = partial[core * n_half + i] + pair_in[i]
+        both = partial[core * n_half + i] + pair_in[i]
+        for c in range(n_chip):
+            half[i * n_chip + c, 0:chip_rows] = both[c * chip_rows : (c + 1) * chip_rows]
 
     keeps = my_aux // n_half == core
-    other = jnp.where(keeps, 0, 1)
     copies = []
     for k in range(n_half):
         place = lax.rem(my_aux + k, n_half)
-        copies.append(
-            pltpu.make_async_remote_copy(
-                src_ref=half.at[place],
-                dst_ref=partial_in.at[my_aux],
-                send_sem=aux_send.at[k],
-                recv_sem=aux_recv.at[k + n_half * other],
-                device_id={"aux": core * n_half + place},
-                device_id_type=MESH,
+        for c in range(n_chip):
+            column = lax.rem(chip + c, n_chip)
+            copies.append(
+                pltpu.make_async_remote_copy(
+                    src_ref=half.at[place * n_chip + column],
+                    dst_ref=partial_in.at[my_aux * n_chip + chip],
+                    send_sem=aux_send,
+                    recv_sem=aux_recv,
+                    device_id={"aux": core * n_half + place, "bas": 2 * column + core},
+                    device_id_type=MESH,
+                )
             )
-        )
-    for k in range(1, n_half):
-        copies[k].start()
+    for copy in copies[1:]:
+        copy.start()
+
+    def counted(number):
+        return pltpu.make_async_remote_copy(
+            src_ref=partial_in.at[pl.ds(0, number)],
+            dst_ref=partial_in.at[pl.ds(0, number)],
+            send_sem=aux_send,
+            recv_sem=aux_recv,
+            device_id={"bas": sibling},
+            device_id_type=MESH,
+        )
+
+    last = pltpu.make_async_remote_copy(
+        src_ref=summed,
+        dst_ref=summed_in,
+        send_sem=bas_send,
+        recv_sem=bas_recv,
+        device_id={"bas": sibling},
+        device_id_type=MESH,
+    )
+
+    @pl.when(keeps)
+    def _():
+        partial_in[my_aux * n_chip + chip] = half[lax.rem(my_aux, n_half) * n_chip + chip]
+        counted(n_aux * n_chip - 1).wait_recv()
+        total = partial_in[0]
+        for a in range(1, n_aux * n_chip):
+            total = total + partial_in[a]
+        upper, lower = total[0:own_rows], total[own_rows:chip_rows]
+        summed[0:own_rows] = jnp.where(core == 0, lower, upper)
+        last.start()
+        out_ref[...] = jnp.where(core == 0, upper, lower)
+        counted(n_half * n_chip - 1).wait_send()
+        last.wait_send()
 
     @pl.when(jnp.logical_not(keeps))
     def _():
         copies[0].start()
-        for copy in copies:
-            copy.wait_send()
-
-    @pl.when(keeps)
-    def _():
-        partial_in[my_aux] = half[lax.rem(my_aux, n_half)]
-        for k in range(1, n_aux):
-            pltpu.make_async_remote_copy(
-                src_ref=half.at[0],
-                dst_ref=partial_in.at[0],
-                send_sem=aux_send.at[0],
-                recv_sem=aux_recv.at[k],
-                device_id={"aux": my_aux},
-                device_id_type=MESH,
-            ).wait_recv()
-        for k in range(1, n_half):
-            copies[k].wait_send()
-        total = partial_in[0]
-        for a in range(1, n_aux):
-            total = total + partial_in[a]
-        for d in range(n_bas):
-            summed[d, 0:own_rows] = total[d * own_rows : (d + 1) * own_rows]
-        summed_in[me] = summed[me]
-
-    copies = []
-    for k in range(1, n_bas):
-        peer = lax.rem(me + k, n_bas)
-        copies.append(
-            pltpu.make_async_remote_copy(
-                src_ref=summed.at[peer],
-                dst_ref=summed_in.at[me],
-                send_sem=bas_send.at[k],
-                recv_sem=bas_recv.at[k],
-                device_id={"bas": peer},
-                device_id_type=MESH,
-            )
-        )
-
-    @pl.when(keeps)
-    def _():
-        for copy in copies:
-            copy.start()
-
-    giver = my_aux // n_half
-    for k in range(1, n_bas):
-
-        @pl.when(lax.rem(me + n_bas - k, 2) == giver)
-        def _(k=k):
-            copies[k - 1].wait_recv()
-
-    total = summed_in[giver]
-    for d in range(2, n_bas, 2):
-        total = total + summed_in[giver + d]
-    out_ref[...] = total[0:own_rows]
-
-    @pl.when(keeps)
-    def _():
-        for copy in copies:
-            copy.wait_send()
-
-    for copy in flag_copies:
-        copy.wait()
-    flagged = flag_in[0]
-    for a in range(1, n_aux):
-        flagged = jnp.maximum(flagged, flag_in[a])
+        counted(n_half * n_chip).wait_send()
+        last.wait_recv()
+        out_ref[...] = summed_in[0:own_rows]
+
     flag_out[...] = flagged
     local = pltpu.make_async_copy(flag_out, flag_smem, flag_local)
     local.start()
@@ -527,10 +511,10 @@
             pltpu.VMEM((window - square, window - square), f32),
             pltpu.VMEM((n_aux, aux_rows, window), f32),
             pltpu.VMEM((n_aux // 2, aux_rows, window), f32),
-            pltpu.VMEM((n_aux // 2, aux_rows, window), f32),
-            pltpu.VMEM((n_aux, aux_rows, window), f32),
-            pltpu.VMEM((n_bas, 8, window), f32),
-            pltpu.VMEM((n_bas, 8, window), f32),
+            pltpu.VMEM((n_aux // 2 * n_bas // 2, 8, window), f32),
+            pltpu.VMEM((n_aux * n_bas // 2, 8, window), f32),
+            pltpu.VMEM((8, window), f32),
+            pltpu.VMEM((8, window), f32),
             pltpu.VMEM((8, 128), i32),
             pltpu.VMEM((n_bas, 8, 128), i32),
             pltpu.SMEM((n_bas, 8, 128), i32),
@@ -554,10 +538,10 @@
             dma,
             dma,
             dma,
-            dma((n_aux,)),
-            dma((n_aux,)),
-            dma((n_bas,)),
-            dma((n_bas,)),
+            dma,
+            dma,
+            dma,
+            dma,
         ],
         compiler_params=pltpu.CompilerParams(
             collective_id=0, has_side_effects=True, vmem_limit_bytes=60 * 2**20

time: 120 us -> 119 us (level)
  no operation moved by 1% of the time
where the time goes in v4:
time: 119 us
  Pallas kernels  117 us (98%)
    pallas_call x1, Pallas kernels, body(): pl.pallas_call(functools.partial(kernel, n_aux, n_bas, tiles, blocks), ou...  117 us

profile of v4, /device:TPU:1, one launch (start us, length us, event | category | flops | bytes accessed | tf_op | source)
XLA Modules:
  0.0 119.0 jit_solution(1722996386244855529)
XLA Ops:
  0.0 0.0 copy-start
  0.0 0.0 copy-start.1
  0.0 0.0 copy-start.2
  0.0 117.5 %exchange.1 = (f32[3,384]{1,0:T(4,128)S(1)}, s32[1,1]{1,0:T(1,128)}) custom-call(s32[3,15]{1,0:T(4,128)} %bitcast.37, s32[3,15]{1,0:T(4,128)} %bitcast.38, s32[3,64]{1,0:T(4,128)} %bitcast.39, bf16[64,128]{1,0:T(8,128)(2,1)} %bitcast.36, bf16[15,128,3,16,128]{4,3,2,1,0:T(8,128)(2,1)} %bitcast.29), custom_call_target="tpu_custom_call" | custom-call | tf_op jit(solution)/shard_map/exchange/pallas_call | solution.py:486
  118.2 0.0 copy-done
  118.2 0.0 copy-done.1
  118.2 0.0 copy-done.2
  118.2 0.2 conditional.1
  118.4 0.6 copy.34
Async XLA Ops:
  0.0 118.2 %copy-start = (bf16[128,64]{0,1:T(8,128)(2,1)S(1)}, bf16[128,64]{0,1:T(8,128)(2,1)}, u32[]{:S(2)}) copy-start(bf16[128,64]{0,1:T(8,128)(2,1)} %param.7) | copy-start | bytes 49156
  0.0 118.2 %copy-start.1 = (s32[15,3]{0,1:T(4,128)S(1)}, s32[15,3]{0,1:T(4,128)}, u32[]{:S(2)}) copy-start(s32[15,3]{0,1:T(4,128)} %param.9) | copy-start | bytes 544
  0.0 118.2 %copy-start.2 = (s32[64,3]{0,1:T(4,128)S(1)}, s32[64,3]{0,1:T(4,128)}, u32[]{:S(2)}) copy-start(s32[64,3]{0,1:T(4,128)} %param.8) | copy-start | bytes 2308

commit v5 on v4

--- a/solution.py
+++ b/solution.py
@@ -1,4 +1,5 @@
 import functools
+import math
 
 import jax
 import jax.numpy as jnp
@@ -15,8 +16,8 @@
 
 CAP = 31
 SPARE = 8
-STAGES = (3, 4, 4, 4, 4, 4, 4, 4)
-HANDOVER_AFTER = 1
+STAGES = (1, 2, 4, 4, 4, 4, 4, 4, 4)
+HANDOVER_AFTER = 3
 HEAD = 3
 HEAD_TILES = 4
 EARLY_TILES = 9
@@ -78,6 +79,8 @@
     pattern_in,
     pattern_all,
     flag_out,
+    flag_row,
+    flag_mid,
     flag_in,
     flag_smem,
     following,
@@ -121,10 +124,12 @@
         pl.semaphore_signal(
             barrier, inc=1, device_id={"bas": lax.rem(me + k, n_bas)}, device_id_type=MESH
         )
-    for k in range(1, n_aux):
-        pl.semaphore_signal(
-            barrier, inc=1, device_id={"aux": lax.rem(my_aux + k, n_aux)}, device_id_type=MESH
-        )
+    side = math.isqrt(n_aux)
+    across, along = my_aux // side, lax.rem(my_aux, side)
+    row_peers = [across * side + lax.rem(along + k, side) for k in range(1, side)]
+    column_peers = [lax.rem(across + k, side) * side + along for k in range(1, side)]
+    for peer in row_peers + column_peers:
+        pl.semaphore_signal(barrier, inc=1, device_id={"aux": peer}, device_id_type=MESH)
 
     following[count] = jnp.int32(count - 1)
     upcoming = jnp.int32(count - 1)
@@ -210,7 +215,7 @@
 
         lax.fori_loop(first, first + size, fill, 0)
         if stage == 0:
-            pl.semaphore_wait(barrier, n_bas + n_aux - 2)
+            pl.semaphore_wait(barrier, n_bas + 2 * side - 3)
 
             pattern_copies = []
             for k in range(1, n_bas):
@@ -225,7 +230,7 @@
                     )
                 )
                 pattern_copies[-1].start()
-        for k in range(1, n_bas):
+        for k in sorted(range(1, n_bas), key=lambda k: abs(k - n_bas // 2)):
             peer = lax.rem(me + k, n_bas)
             where = (recv_early, first) if first < EARLY else (recv_late, first - EARLY)
             copies.append(
@@ -292,20 +297,24 @@
     for d in range(n_bas):
         over = jnp.where(counts[d] > CAP + SPARE, 1, over)
     flag_out[...] = jnp.full(flag_out.shape, over, jnp.int32)
-    flag_copies = []
-    for k in range(1, n_aux):
-        flag_copies.append(
+
+    def pass_flag(flag, landing, place, peers, lane):
+        return [
             pltpu.make_async_remote_copy(
-                src_ref=flag_out,
-                dst_ref=flag_in.at[my_aux],
-                send_sem=flag_send.at[k],
-                recv_sem=flag_recv.at[k],
-                device_id={"aux": lax.rem(my_aux + k, n_aux)},
+                src_ref=flag,
+                dst_ref=landing.at[place],
+                send_sem=flag_send.at[lane + k],
+                recv_sem=flag_recv.at[lane + k],
+                device_id={"aux": peer},
                 device_id_type=MESH,
             )
-        )
-        flag_copies[-1].start()
-    flag_in[my_aux] = flag_out[...]
+            for k, peer in enumerate(peers)
+        ]
+
+    flag_copies = pass_flag(flag_out, flag_row, along, row_peers, 0)
+    for copy in flag_copies:
+        copy.start()
+    flag_row[along] = flag_out[...]
 
     span_rows = n_bas * blocks * BAS_TILE
     aux_rows = span_rows // n_aux
@@ -356,6 +365,16 @@
     ranks = (jnp.int32(0),) * n_bas
     for stage, size in enumerate(STAGES):
         if first == EARLY:
+            for copy in flag_copies:
+                copy.wait()
+            flagged = flag_row[0]
+            for a in range(1, side):
+                flagged = jnp.maximum(flagged, flag_row[a])
+            flag_mid[...] = flagged
+            flag_copies = pass_flag(flag_mid, flag_in, across, column_peers, side)
+            for copy in flag_copies:
+                copy.start()
+            flag_in[across] = flag_mid[...]
             owns[0].wait()
             ranks = lax.fori_loop(
                 0, EARLY_TILES // GROUP, functools.partial(gram, late=False), ranks
@@ -384,7 +403,7 @@
     for copy in flag_copies:
         copy.wait()
     flagged = flag_in[0]
-    for a in range(1, n_aux):
+    for a in range(1, side):
         flagged = jnp.maximum(flagged, flag_in[a])
 
     core = lax.rem(me, 2)
@@ -480,6 +499,7 @@
     aux_rows = window // n_aux
     own_rows = aux_rows // n_bas
     square = window // 3 * 2
+    side = math.isqrt(n_aux)
     vmem = pl.BlockSpec(memory_space=pltpu.VMEM)
     dma = pltpu.SemaphoreType.DMA
     bf16, f32, i32 = jnp.bfloat16, jnp.float32, jnp.int32
@@ -519,7 +539,9 @@
             pltpu.VMEM((n_bas, 8, 128), i32),
             pltpu.SMEM((n_bas, 8, 128), i32),
             pltpu.VMEM((8, 128), i32),
-            pltpu.VMEM((n_aux, 8, 128), i32),
+            pltpu.VMEM((side, 8, 128), i32),
+            pltpu.VMEM((8, 128), i32),
+            pltpu.VMEM((side, 8, 128), i32),
             pltpu.SMEM((8, 128), i32),
             pltpu.SMEM((tiles * blocks + 1,), i32),
             pltpu.SMEM((CAP + SPARE,), i32),
@@ -533,8 +555,8 @@
             dma((2,)),
             dma,
             dma,
-            dma((n_aux,)),
-            dma((n_aux,)),
+            dma((2 * side,)),
+            dma((2 * side,)),
             dma,
             dma,
             dma,

time: 119 us -> 119 us (level)
  no operation moved by 1% of the time
where the time goes in v5:
time: 119 us; the launch traced here: 118 us
  Pallas kernels  117 us (98%)
    pallas_call x1, Pallas kernels, body(): pl.pallas_call(functools.partial(kernel, n_aux, n_bas, tiles, blocks), ou...  117 us

profile of v5, /device:TPU:1, one launch (start us, length us, event | category | flops | bytes accessed | tf_op | source)
XLA Modules:
  0.0 118.4 jit_solution(18171880778597896753)
XLA Ops:
  0.0 0.0 copy-start
  0.0 0.0 copy-start.1
  0.0 0.0 copy-start.2
  0.0 116.8 %exchange.1 = (f32[3,384]{1,0:T(4,128)S(1)}, s32[1,1]{1,0:T(1,128)}) custom-call(s32[3,15]{1,0:T(4,128)} %bitcast.37, s32[3,15]{1,0:T(4,128)} %bitcast.38, s32[3,64]{1,0:T(4,128)} %bitcast.39, bf16[64,128]{1,0:T(8,128)(2,1)} %bitcast.36, bf16[15,128,3,16,128]{4,3,2,1,0:T(8,128)(2,1)} %bitcast.29), custom_call_target="tpu_custom_call" | custom-call | tf_op jit(solution)/shard_map/exchange/pallas_call | solution.py:506
  117.5 0.0 copy-done
  117.5 0.0 copy-done.1
  117.6 0.0 copy-done.2
  117.6 0.2 conditional.1
  117.8 0.6 copy.34
Async XLA Ops:
  0.0 117.5 %copy-start = (bf16[128,64]{0,1:T(8,128)(2,1)S(1)}, bf16[128,64]{0,1:T(8,128)(2,1)}, u32[]{:S(2)}) copy-start(bf16[128,64]{0,1:T(8,128)(2,1)} %param.7) | copy-start | bytes 49156
  0.0 117.5 %copy-start.1 = (s32[15,3]{0,1:T(4,128)S(1)}, s32[15,3]{0,1:T(4,128)}, u32[]{:S(2)}) copy-start(s32[15,3]{0,1:T(4,128)} %param.9) | copy-start | bytes 544
  0.0 117.6 %copy-start.2 = (s32[64,3]{0,1:T(4,128)S(1)}, s32[64,3]{0,1:T(4,128)}, u32[]{:S(2)}) copy-start(s32[64,3]{0,1:T(4,128)} %param.8) | copy-start | bytes 2308
